TPU v7x, 512 devices: a whole 4x4x16 slice. The times are simulated.
512 devices in a mesh: gx: 128 (over z, y, core), gy: 4 (over x).
Axes of the slice: x: 4, y: 4, z: 16, core: 2. Of those that a mesh axis runs over, the one named last changes fastest.
Arguments:
- x_data: float32 [256, 256, 256, 16], P('gx', None, 'gy'), as said below
- start_x: float32 [256, 64], replicated, may hold values from -6 to 6
- start_y: float32 [256, 64], replicated, may hold values from -6 to 6
- start_z: float32 [256, 64], replicated, may hold values from -6 to 6
Outputs:
- core: float32 [1024, 64, 64], P('gx', 'gy')
- factor_x: float32 [256, 64], replicated
- factor_y: float32 [256, 64], replicated
- factor_z: float32 [256, 64], replicated
Inputs may be any that keep to these rules, and one draw needn't show every extreme that they name: `x_data`: real-valued field samples.
All inputs are finite; a program needn't handle non-finite values.
Results may differ from a plain program's by a relative error of at most 0.0003.
Values sent between devices are 32-bit elements; how exact they have to be, the bound alone decides.
A program may use at most 64 MiB of HBM per device.

v0:
```python
import jax
import jax.numpy as jnp
from jax import lax
from jax.sharding import PartitionSpec as P

ITERS = 4


def local_gram(columns):
    return lax.dot_general(
        columns, columns, (((1,), (1,)), ((), ())), precision=lax.Precision.HIGHEST
    )


def orthonormal(image):
    inner = jnp.dot(image.T, image, precision=lax.Precision.HIGHEST)
    lower = jnp.linalg.cholesky(inner)
    return jax.scipy.linalg.solve_triangular(lower, image.T, lower=True).T


def solve_factor(partial_gram, start):
    block = start
    total = lax.psum(partial_gram, ("gx", "gy"))
    for step in range(ITERS):
        image = jnp.dot(total, block, precision=lax.Precision.HIGHEST)
        block = orthonormal(image)
    return block


def local(x_data, start_x, start_y, start_z):
    high = lax.Precision.HIGHEST
    x_local, z_count, y_local, species = x_data.shape
    gx_count = lax.axis_size("gx")
    gy_count = lax.axis_size("gy")
    x_count = x_local * gx_count
    z_local = z_count // gx_count
    y_count = y_local * gy_count
    rank = start_x.shape[1]
    rank_local = rank // gy_count
    x_lines = lax.all_to_all(
        x_data.reshape(x_local, z_count, y_local * species),
        "gx",
        split_axis=1,
        concat_axis=0,
        tiled=True,
    )
    factor_x = solve_factor(
        local_gram(x_lines.reshape(x_count, z_local * y_local * species)), start_x
    )
    first_core = jnp.einsum(
        "xk,xzys->ykzs",
        factor_x,
        x_lines.reshape(x_count, z_local, y_local, species),
        precision=high,
    )
    y_lines = lax.all_to_all(
        first_core.reshape(y_local, rank * z_local * species),
        "gy",
        split_axis=1,
        concat_axis=0,
        tiled=True,
    )
    factor_y = solve_factor(local_gram(y_lines), start_y)
    second_core = jnp.einsum(
        "yl,yazs->zlsa",
        factor_y,
        y_lines.reshape(y_count, rank_local, z_local, species),
        precision=high,
    )
    z_lines = lax.all_to_all(
        second_core.reshape(z_local, rank * species * rank_local),
        "gx",
        split_axis=1,
        concat_axis=0,
        tiled=True,
    )
    factor_z = solve_factor(local_gram(z_lines), start_z)
    z_count_all = z_lines.shape[0]
    core = jnp.einsum(
        "zm,zpa->pam", factor_z, z_lines.reshape(z_count_all, -1, rank_local), precision=high
    )
    return (core, factor_x, factor_y, factor_z)


def solution(mesh):
    placed = (P("gx", None, "gy", None), P(), P(), P())
    return jax.shard_map(
        local,
        mesh=mesh,
        in_specs=placed,
        out_specs=(P("gx", "gy", None), P(), P(), P()),
        check_vma=False,
    )
```

profile of v0, /device:TPU:1, one launch (start us, length us, event | category | flops | bytes accessed | tf_op | source)
XLA Modules:
  0.0 1703.7 jit_solution(16642359762633729425)
XLA Ops:
  7.2 2.9 copy.43
  10.2 117.2 %all_to_all.53 = f32[2,256,1024]{2,0,1:T(2,128)S(1)} all-to-all(f32[2,256,1024]{2,0,1:T(2,128)S(1)} %copy.43), channel_id=1, replica_groups=mesh['gx'=128,'gy'=4] {'gx'}, dimensions={1} | all-to-all | bytes 4194304 | tf_op jit(solution)/shard_map/all_to_all | solution.py:40
  127.4 1.1 copy.44
  128.5 0.9 copy.67
  129.4 2.6 fusion.71
  132.0 9.0 reshape.47
  141.0 12.8 copy.50
  153.8 428.9 %all-reduce.4.cloned.1.call-done = f32[256,256]{1,0:T(8,128)} async-done(((f32[256,256]{1,0:T(8,128)}), f32[256,256]{1,0:T(8,128)}) %all-reduce.4.cloned.1.call-update) | async-done | bytes 262160 | tf_op jit(solution)/shard_map/psum | solution.py:23
  582.7 1.4 fusion.72
  584.4 5.8 cholesky.194
  590.3 0.6 compare_reduce_fusion.11
  590.9 0.7 fusion.29
  591.6 4.9 custom-call.16
  596.7 1.3 fusion.74
  598.4 5.8 cholesky.205
  604.3 0.6 compare_reduce_fusion.10
  604.9 0.7 fusion.30
  605.6 4.9 custom-call.17
  611.4 5.8 cholesky.216
  617.3 0.6 compare_reduce_fusion.9
  618.0 0.7 fusion.31
  618.6 4.9 custom-call.18
  624.5 5.8 cholesky.227
  630.4 0.6 compare_reduce_fusion.8
  631.0 0.7 fusion.32
  631.7 4.9 custom-call.19
  636.8 3.2 convolution_bitcast_fusion
  641.1 10.8 all_to_all.54
  652.0 1.3 fusion.80
  654.4 453.2 %all-reduce.6.cloned.1.call-done = f32[256,256]{1,0:T(8,128)} async-done(((f32[256,256]{1,0:T(8,128)}), f32[256,256]{1,0:T(8,128)}) %all-reduce.6.cloned.1.call-update) | async-done | bytes 262160 | tf_op jit(solution)/shard_map/psum | solution.py:23
  1107.6 1.4 fusion.81
  1109.3 5.8 cholesky.238
  1115.1 0.6 compare_reduce_fusion.7
  1115.8 0.7 fusion.33
  1116.4 4.9 custom-call.20
  1121.6 1.3 fusion.83
  1123.2 5.8 cholesky.249
  1129.1 0.6 compare_reduce_fusion.6
  1129.8 0.7 fusion.34
  1130.4 4.9 custom-call.21
  1136.3 5.8 cholesky.260
  1142.8 0.7 fusion.35
  1143.5 4.9 custom-call.22
  1149.3 5.8 cholesky.271
  1155.9 0.7 fusion.36
  1156.5 4.9 custom-call.23
  1163.3 30.0 %all_to_all.55 = f32[2,128,128]{2,0,1:T(2,128)S(1)} all-to-all(f32[2,128,128]{2,0,1:T(2,128)S(1)} %copy.59), channel_id=1, replica_groups=mesh['gx'=128,'gy'=4] {'gx'}, dimensions={1} | all-to-all | bytes 262144 | tf_op jit(solution)/shard_map/all_to_all | solution.py:70
  1193.2 1.1 fusion.89
  1194.7 445.7 %all-reduce.8.cloned.1.call-done = f32[256,256]{1,0:T(8,128)} async-done(((f32[256,256]{1,0:T(8,128)}), f32[256,256]{1,0:T(8,128)}) %all-reduce.8.cloned.1.call-update) | async-done | bytes 262160 | tf_op jit(solution)/shard_map/psum | solution.py:23
  1640.4 1.4 fusion.90
  1642.1 5.8 cholesky.282
  1648.6 0.7 fusion.37
  1649.3 4.9 custom-call.24
  1654.5 1.3 fusion.92
  1656.1 5.8 cholesky.293
  1662.6 0.7 fusion.38
  1663.3 4.9 custom-call.25
  1669.1 5.8 cholesky.304
  1675.7 0.7 fusion.39
  1676.3 4.9 custom-call.26
  1682.2 5.8 cholesky.315
  1688.7 0.7 fusion.40
  1689.4 4.9 custom-call.27
  1694.6 2.4 fusion
  (105 shorter events, 17.4 us)
Async XLA Ops:
  7.2 575.5 %copy-start = (f32[256,64]{0,1:T(8,128)S(1)}, f32[256,64]{0,1:T(8,128)}, u32[]{:S(2)}) copy-start(f32[256,64]{0,1:T(8,128)} %param.8) | copy-start | bytes 196612
  7.2 575.5 %all-reduce.4.cloned.1.call-start = ((), (), s32[]{:S(2)}) async-start(), calls=%async_computation.3 | async-start | bytes 524288 | tf_op jit(solution)/shard_map/psum | solution.py:23
  132.0 975.6 %all-reduce.6.cloned.1.call-start = ((), (), s32[]{:S(2)}) async-start(), calls=%async_computation.4 | async-start | bytes 524288 | tf_op jit(solution)/shard_map/psum | solution.py:23
  582.7 28.1 %copy-start.1 = (f32[256,256]{1,0:T(8,128)S(1)}, f32[256,256]{1,0:T(8,128)}, u32[]{:S(2)}) copy-start(f32[256,256]{1,0:T(8,128)} %all-reduce.4.cloned.1.call-done) | copy-start | bytes 786436
  636.8 3.8 copy-start.4
  652.0 455.6 %copy-start.7 = (f32[256,64]{0,1:T(8,128)S(1)}, f32[256,64]{0,1:T(8,128)}, u32[]{:S(2)}) copy-start(f32[256,64]{0,1:T(8,128)} %param.9) | copy-start | bytes 196612
  653.3 987.1 %all-reduce.8.cloned.1.call-start = ((), (), s32[]{:S(2)}) async-start(), calls=%async_computation.5 | async-start | bytes 524288 | tf_op jit(solution)/shard_map/psum | solution.py:23
  1107.6 28.1 %copy-start.2 = (f32[256,256]{1,0:T(8,128)S(1)}, f32[256,256]{1,0:T(8,128)}, u32[]{:S(2)}) copy-start(f32[256,256]{1,0:T(8,128)} %all-reduce.6.cloned.1.call-done) | copy-start | bytes 786436
  1161.7 32.6 %copy-start.6 = (f32[64,256]{1,0:T(8,128)}, f32[64,256]{1,0:T(8,128)S(1)}, u32[]{:S(2)}) copy-start(f32[64,256]{1,0:T(8,128)S(1)} %fusion.13) | copy-start | bytes 196612
  1162.8 477.5 %copy-start.8 = (f32[256,64]{0,1:T(8,128)S(1)}, f32[256,64]{0,1:T(8,128)}, u32[]{:S(2)}) copy-start(f32[256,64]{0,1:T(8,128)} %param.10) | copy-start | bytes 196612
  1640.4 28.1 %copy-start.3 = (f32[256,256]{1,0:T(8,128)S(1)}, f32[256,256]{1,0:T(8,128)}, u32[]{:S(2)}) copy-start(f32[256,256]{1,0:T(8,128)} %all-reduce.8.cloned.1.call-done) | copy-start | bytes 786436
  1694.6 2.4 copy-start.5
Sparse Core Ops, SparseCore 0:
  132.1 450.5 all-reduce.3
  653.4 454.0 all-reduce.5
  1194.5 445.8 all-reduce.7
where the time goes:
time: 1710 us; the launch traced here: 1700 us
  waiting for transfers between devices  1330 us (78%)
  blocking collectives  158 us (9%)
  other arithmetic  145 us (8%)
  local copies, waits for them, and re-layouts  31.1 us (2%)
  matrix products  27.2 us (2%)
    psum x3, waiting for transfers between devices, solve_factor(): total = lax.psum(partial_gram, ('gx', 'gy'))  1330 us
    all_to_all x1, blocking collectives, local(): lax.all_to_all(x_data.reshape(x_local, z_count, y_local * species), 'gx',...  117 us
    another operation x36, other arithmetic, orthonormal(): lower = jnp.linalg.cholesky(inner)  78.2 us
    another operation x24, other arithmetic, orthonormal(): return jax.scipy.linalg.solve_triangular(lower, image.T, lower=True).T  66.6 us
  transfers between devices with their start and end apart: 3, of which 3 were waited for; matrix products, arithmetic and copies ran while one was open for 1% of the time, Pallas kernels for 0%

commit v1 on v0

v1 whole, which is shorter than its diff:
```python
import functools

import jax
import jax.numpy as jnp
from jax import lax
from jax.experimental import pallas as pl
from jax.experimental.pallas import tpu as pltpu
from jax.sharding import PartitionSpec as P

ITERS = 4
MESH = pl.DeviceIdType.MESH
HIGHEST = lax.Precision.HIGHEST
Z_STEPS = [8] + [sign * d for d in range(7, 0, -1) for sign in (1, -1)]


def dot(a, b, ca, cb):
    return lax.dot_general(
        a, b, (((ca,), (cb,)), ((), ())), precision=HIGHEST, preferred_element_type=jnp.float32
    )


def position():
    g = lax.axis_index("gx")
    return lax.axis_index("gy"), (g // 2) % 4, g // 8, g % 2


def device(x, y, z, c):
    return ((z * 4 + y) * 2 + c, x)


def plane_index(x, y, c):
    return (y * 2 + c) * 4 + x


def plane_peer(i, x, y, c):
    return (x + i % 4) % 4, (y + i // 8) % 4, (c + (i // 4) % 2) % 2


def inverse_cholesky(p):
    n = 64
    row = lax.broadcasted_iota(jnp.int32, (n, n), 0)
    col = lax.broadcasted_iota(jnp.int32, (n, n), 1)
    m = jnp.concatenate([p, (row == col).astype(jnp.float32)], axis=1)
    sub = lax.broadcasted_iota(jnp.int32, (8, 128), 0)
    blocks = [m[8 * i : 8 * i + 8, :] for i in range(8)]
    out = []
    for k in range(8):
        cols = {
            (i, j): jnp.broadcast_to(blocks[i][:, 8 * k + j : 8 * k + j + 1], (8, 128))
            for j in range(8)
            for i in range(k, 8)
        }
        rows = [jnp.broadcast_to(blocks[k][j : j + 1, :], (8, 128)) for j in range(8)]
        splat = {
            (r, j): jnp.broadcast_to(cols[k, j][r : r + 1, :], (8, 128))
            for j in range(8)
            for r in range(j, 8)
        }
        for j in range(8):
            scale = lax.rsqrt(splat[j, j])
            for r in range(j + 1, 8):
                splat[r, j] = splat[r, j] * scale
            for i in range(k + 1, 8):
                cols[i, j] = cols[i, j] * scale
            rows[j] = rows[j] * scale
            for t in range(j + 1, 8):
                for r in range(t, 8):
                    splat[r, t] = splat[r, t] - splat[r, j] * splat[t, j]
                for i in range(k + 1, 8):
                    cols[i, t] = cols[i, t] - cols[i, j] * splat[t, j]
                rows[t] = rows[t] - rows[j] * splat[t, j]
        for i in range(k + 1, 8):
            for j in range(8):
                blocks[i] = blocks[i] - cols[i, j] * rows[j]
        done = rows[0]
        for j in range(1, 8):
            done = jnp.where(sub == j, rows[j], done)
        out.append(done)
    return jnp.concatenate(out, axis=0)[:, n:]


def factor(gram, start_t, out_ref):
    out_ref[...] = start_t

    def step(_, carry):
        image = dot(out_ref[...], gram[...], 1, 0)
        inner = dot(image, image, 1, 1)
        out_ref[...] = dot(inverse_cholesky(inner), image, 1, 0)
        return carry

    lax.fori_loop(0, ITERS, step, 0)


def permutation(kind):
    old = lax.broadcasted_iota(jnp.int32, (256, 256), 0)
    new = lax.broadcasted_iota(jnp.int32, (256, 256), 1)
    if kind == "x":
        source = (new % 128) * 2 + new // 128
    else:
        source = (new % 32) * 8 + new // 32
    return (old == source).astype(jnp.float32)


def swap_blocks(parts):
    lane = lax.broadcasted_iota(jnp.int32, (32, 128), 1) // 16
    parts = list(parts)
    for bit in (1, 2, 4):
        high = (lane & bit) != 0
        new = list(parts)
        for a in range(8):
            if a & bit == 0:
                lo, hi = parts[a], parts[a + bit]
                new[a] = jnp.where(high, pltpu.roll(hi, 16 * bit, 1), lo)
                new[a + bit] = jnp.where(high, hi, pltpu.roll(lo, 128 - 16 * bit, 1))
        parts = new
    return parts


def all_reduce(gram, r1, r2, part, out, sems):
    x, y, z, c = position()
    own = plane_index(x, y, c)

    def send_rows(i, carry):
        tx, ty, tc = plane_peer(i, x, y, c)
        rows = pl.ds(pl.multiple_of(plane_index(tx, ty, tc) * 8, 8), 8)
        pltpu.make_async_remote_copy(
            gram.at[rows, :], r1.at[i], sems.at[0], sems.at[1],
            device_id=device(tx, ty, z, tc), device_id_type=MESH,
        ).start()
        return carry

    for i in range(1, 32):
        send_rows(i, 0)
    mine = pl.ds(pl.multiple_of(own * 8, 8), 8)
    total = gram[mine, :]
    others = r1.at[pl.ds(1, 31)]
    pltpu.make_async_copy(others, others, sems.at[1]).wait()
    for i in range(1, 32):
        total = total + r1[i]
    part[0] = total
    r2[z] = total
    for dz in Z_STEPS:
        pltpu.make_async_remote_copy(
            part.at[0], r2.at[z], sems.at[2], sems.at[3],
            device_id=device(x, y, (z + dz + 16) % 16, c), device_id_type=MESH,
        ).start()
    fifteen = r1.at[pl.ds(1, 15)]
    pltpu.make_async_copy(fifteen, fifteen, sems.at[3]).wait()
    total = r2[0]
    for i in range(1, 16):
        total = total + r2[i]
    part[1] = total
    out[mine, :] = total
    for i in range(1, 32):
        tx, ty, tc = plane_peer(i, x, y, c)
        pltpu.make_async_remote_copy(
            part.at[1], out.at[mine, :], sems.at[4], sems.at[5],
            device_id=device(tx, ty, z, tc), device_id_type=MESH,
        ).start()
    pltpu.make_async_copy(others, others, sems.at[5]).wait()
    pltpu.make_async_copy(others, others, sems.at[0]).wait()
    pltpu.make_async_copy(fifteen, fifteen, sems.at[2]).wait()
    pltpu.make_async_copy(others, others, sems.at[4]).wait()


def kernel(
    xt, sx, sy, sz, core, fx, fy, fz,
    outgoing, by_z, lines, matrix, fc, sc, q, d, at, perm_x, perm_z, vt, halves, gram, total, r1, r2, part,
    ar_sems, z_recv, sems,
):
    x, y, z, c = position()
    own = plane_index(x, y, c)
    barrier = pltpu.get_barrier_semaphore()
    for i in range(1, 32):
        tx, ty, tc = plane_peer(i, x, y, c)
        pl.semaphore_signal(barrier, 1, device_id=device(tx, ty, z, tc), device_id_type=MESH)
    for dz in range(1, 16):
        for dc in range(2):
            pl.semaphore_signal(
                barrier, 1, device_id=device(x, y, (z + dz) % 16, (c + dc) % 2), device_id_type=MESH
            )

    sub = lax.broadcasted_iota(jnp.int32, (8, 128), 0)
    lane = lax.broadcasted_iota(jnp.int32, (8, 128), 1)
    keep = (sub < 4) == (lane < 64)

    def turn(half, carry):
        for s in range(16):
            t = xt[:, s, pl.ds(pl.multiple_of(half * 128, 128), 128)].T
            for zb in range(16):
                tile = t[zb * 8 : zb * 8 + 8, :]
                moved = pltpu.roll(pltpu.roll(tile, 4, 0), 64, 1)
                outgoing[s, half * 16 + zb] = jnp.where(keep, tile, moved)
        return carry

    lax.fori_loop(0, 2, turn, 0)
    perm_x[...] = permutation("x")
    perm_z[...] = permutation("z")
    vt[0] = dot(sx[...], perm_x[...], 1, 0)
    vt[1] = dot(sz[...], perm_z[...], 1, 0)

    pl.semaphore_wait(barrier, 61)

    for k, dz in enumerate(Z_STEPS):
        tz = (z + dz + 16) % 16
        pltpu.make_async_remote_copy(
            outgoing.at[tz], by_z.at[z], sems.at[0], z_recv.at[k],
            device_id=device(x, y, tz, c), device_id_type=MESH,
        ).start()

    yc = y * 2 + c

    def forward(buffer, zs, slot):
        def one(i, carry):
            tx, ty, tc = plane_peer(i, x, y, c)
            pltpu.make_async_remote_copy(
                buffer.at[slot, plane_index(tx, ty, tc)], lines.at[x, zs * 8 + yc],
                sems.at[1], sems.at[2],
                device_id=device(tx, ty, z, tc), device_id_type=MESH,
            ).start()
            return carry

        lax.fori_loop(1, 32, one, 0)
        lines[x, zs * 8 + yc] = buffer[slot, own]

    forward(outgoing, z, z)
    for k, dz in enumerate(Z_STEPS):
        arrived = by_z.at[0]
        pltpu.make_async_copy(arrived, arrived, z_recv.at[k]).wait()
        zs = (z - dz + 16) % 16
        forward(by_z, zs, zs)
    most = outgoing.at[pl.ds(0, 15)]
    pltpu.make_async_copy(most, most, sems.at[0]).wait()
    tiles = outgoing.at[:, pl.ds(0, 31)]
    pltpu.make_async_copy(tiles, tiles, sems.at[2]).wait()
    pltpu.make_async_copy(tiles, tiles, sems.at[1]).wait()

    for cx in range(4):
        for zh in range(4):
            for p in range(2):
                matrix[p * 128 : p * 128 + 128, (cx * 4 + zh) * 128 : (cx * 4 + zh + 1) * 128] = (
                    lines[cx, :, p * 4 + zh, :]
                )
    gram[...] = dot(matrix[...], matrix[...], 1, 1)
    all_reduce(gram, r1.at[0], r2.at[0], part.at[0], total.at[0], ar_sems.at[0])
    factor(total.at[0], vt[0], vt.at[2])
    fx[...] = dot(vt[2], perm_x[...], 1, 1)

    low = lax.broadcasted_iota(jnp.int32, (64, 128), 1) < 64
    for zh in range(4):
        piece = [
            dot(vt[2], matrix[:, (cx * 4 + zh) * 128 : (cx * 4 + zh + 1) * 128], 1, 0)
            for cx in range(4)
        ]
        turned = [pltpu.roll(v, 64, 1) for v in piece]
        for pair in range(2):
            a, b = 2 * pair, 2 * pair + 1
            for zl, value in (
                (0, jnp.where(low, piece[a], turned[b])),
                (1, jnp.where(low, turned[a], piece[b])),
            ):
                zz = zl * 4 + zh
                for kb in range(4):
                    fc[kb * 128 + zz * 16 : kb * 128 + zz * 16 + 16, pair * 128 : pair * 128 + 128] = (
                        value[kb * 16 : kb * 16 + 16, :]
                    )
    gram[...] = dot(fc[...], fc[...], 0, 0)
    all_reduce(gram, r1.at[1], r2.at[1], part.at[1], total.at[1], ar_sems.at[1])
    factor(total.at[1], sy[...], fy)

    for lanes in range(2):
        halves[lanes] = fy[:, lanes * 128 : lanes * 128 + 128]
        for cy in range(4):
            for half in range(2):
                first = (cy * 2 + half) * 8
                vt[2, first : first + 8, lanes * 128 : lanes * 128 + 128] = halves[
                    lanes, pl.ds(32 * half + cy, 8, stride=4), :
                ]
    product = dot(vt[2], fc[...], 1, 1)
    for t in range(8):
        for cx in range(4):
            sc[t * 4 + cx] = product[t * 8 : t * 8 + 8, cx * 128 : cx * 128 + 128]

    for i in range(1, 32):
        tx, ty, tc = plane_peer(i, x, y, c)
        pltpu.make_async_remote_copy(
            sc.at[plane_index(tx, ty, tc)], q.at[own], sems.at[3], sems.at[4],
            device_id=device(tx, ty, z, tc), device_id_type=MESH,
        ).start()
    q[own] = sc[own]
    tiles = sc.at[pl.ds(0, 31)]
    pltpu.make_async_copy(tiles, tiles, sems.at[4]).wait()
    pltpu.make_async_copy(tiles, tiles, sems.at[3]).wait()

    for m in range(8):
        at[1, m * 32 : m * 32 + 32, :] = q[:, m, :]
    tc = z // 8
    for m in range(8):
        tz = c * 8 + m

        @pl.when(jnp.logical_or(tz != z, tc != c))
        def _():
            pltpu.make_async_remote_copy(
                at.at[1, pl.ds(m * 32, 32), :], d.at[z % 8], sems.at[5], sems.at[6],
                device_id=device(x, y, tz, tc), device_id_type=MESH,
            ).start()

        @pl.when(jnp.logical_and(tz == z, tc == c))
        def _():
            d[z % 8] = at[1, m * 32 : m * 32 + 32, :]

    lines_z = swap_blocks([at[1, m * 32 : m * 32 + 32, :] for m in range(8)])
    for zz in range(8):
        at[0, zz * 32 : zz * 32 + 32, :] = lines_z[zz]
    gram[...] = dot(at[0], at[0], 1, 1)
    all_reduce(gram, r1.at[2], r2.at[2], part.at[2], total.at[2], ar_sems.at[2])
    factor(total.at[2], vt[1], vt.at[2])
    fz[...] = dot(vt[2], perm_z[...], 1, 1)

    @pl.when(tc == c)
    def _():
        seven = d.at[pl.ds(0, 7)]
        pltpu.make_async_copy(seven, seven, sems.at[6]).wait()
        pltpu.make_async_copy(seven, seven, sems.at[5]).wait()

    @pl.when(tc != c)
    def _():
        pltpu.make_async_copy(d, d, sems.at[6]).wait()
        pltpu.make_async_copy(d, d, sems.at[5]).wait()

    by_zz = swap_blocks([d[s] for s in range(8)])
    for zz in range(8):
        at[0, zz * 32 : zz * 32 + 32, :] = by_zz[zz]
    result = dot(at[0], vt[2], 0, 1)
    for s in range(8):
        core[s] = result[s * 16 : s * 16 + 16, :]


def local(x_data, start_x, start_y, start_z):
    f32 = jnp.float32
    vmem = pl.BlockSpec(memory_space=pltpu.VMEM)
    xt = jnp.transpose(x_data, (0, 2, 3, 1)).reshape(128, 16, 256)
    core, fx, fy, fz = pl.pallas_call(
        kernel,
        out_shape=[
            jax.ShapeDtypeStruct((8, 16, 64), f32),
            jax.ShapeDtypeStruct((64, 256), f32),
            jax.ShapeDtypeStruct((64, 256), f32),
            jax.ShapeDtypeStruct((64, 256), f32),
        ],
        in_specs=[vmem] * 4,
        out_specs=[vmem] * 4,
        scratch_shapes=[
            pltpu.VMEM((16, 32, 8, 128), f32),
            pltpu.VMEM((16, 32, 8, 128), f32),
            pltpu.VMEM((4, 128, 8, 128), f32),
            pltpu.VMEM((256, 2048), f32),
            pltpu.VMEM((512, 256), f32),
            pltpu.VMEM((32, 8, 128), f32),
            pltpu.VMEM((32, 8, 128), f32),
            pltpu.VMEM((8, 32, 128), f32),
            pltpu.VMEM((2, 256, 128), f32),
            pltpu.VMEM((256, 256), f32),
            pltpu.VMEM((256, 256), f32),
            pltpu.VMEM((3, 64, 256), f32),
            pltpu.VMEM((2, 64, 128), f32),
            pltpu.VMEM((256, 256), f32),
            pltpu.VMEM((3, 256, 256), f32),
            pltpu.VMEM((3, 32, 8, 256), f32),
            pltpu.VMEM((3, 16, 8, 256), f32),
            pltpu.VMEM((3, 2, 8, 256), f32),
            pltpu.SemaphoreType.DMA((3, 6)),
            pltpu.SemaphoreType.DMA((15,)),
            pltpu.SemaphoreType.DMA((7,)),
        ],
        compiler_params=pltpu.CompilerParams(
            collective_id=0, has_side_effects=True, vmem_limit_bytes=40 << 20
        ),
    )(xt, start_x.T, start_y.T, start_z.T)
    return core, fx.T, fy.T, fz.T


def solution(mesh):
    placed = (P("gx", None, "gy", None), P(), P(), P())
    return jax.shard_map(
        local,
        mesh=mesh,
        in_specs=placed,
        out_specs=(P("gx", "gy", None), P(), P(), P()),
        check_vma=False,
    )
```

time: 1710 us -> 235 us (0.14)
  waiting for transfers between devices: 1330 us -> 0 us
  Pallas kernels: 0 us -> 228 us
  blocking collectives: 158 us -> 0 us
  other arithmetic: 145 us -> 0 us
  matrix products: 27.2 us -> 0 us
  local copies, waits for them, and re-layouts: 31.1 us -> 6.62 us
    psum x3 -> x0, waiting for transfers between devices: 1330 us -> none  [solve_factor(): total = lax.psum(partial_gram, ('gx', 'gy'))]
    pallas_call x0 -> x1, Pallas kernels: none -> 228 us  [local(): pl.pallas_call(kernel, out_shape=[jax.ShapeDtypeStruct((8, 16, 64), f32),...]
    all_to_all x3 -> x0, blocking collectives: 158 us -> none  [the longest x1 117 us: local(): lax.all_to_all(x_data.reshape(x_local, z_count, y_local * species), 'gx',...]
    another operation x60 -> x0, other arithmetic: 145 us -> none  [the longest x36 78.2 us: orthonormal(): lower = jnp.linalg.cholesky(inner)]
    reshape x5 -> x0, local copies, waits for them, and re-layouts: 25.7 us -> none  [the longest x2 21.8 us: local(): x_lines.reshape(x_count, z_local, y_local, species)]
    dot_general x30 -> x0, matrix products: 24 us -> none  [the longest x12 10.4 us: solve_factor(): image = jnp.dot(total, block, precision=lax.Precision.HIGHEST)]
  transfers between devices with their start and end apart: 3 -> 0, of which waited for: 3 -> 0; matrix products, arithmetic and copies ran while one was open for 1% -> 0% of each run, Pallas kernels for 0% -> 0%
where the time goes in v1:
time: 235 us
  Pallas kernels  228 us (97%)
  local copies, waits for them, and re-layouts  6.62 us (3%)
    pallas_call x1, Pallas kernels, local(): pl.pallas_call(kernel, out_shape=[jax.ShapeDtypeStruct((8, 16, 64), f32),...  228 us
    unnamed x12, local copies, waits for them, and re-layouts  6.62 us

profile of v1, /device:TPU:1, one launch (start us, length us, event | category | flops | bytes accessed | tf_op | source)
XLA Modules:
  0.0 235.1 jit_solution(12680467786882955959)
XLA Ops:
  0.6 0.0 copy-start
  0.6 1.6 copy-done
  2.2 0.0 copy-start.1
  2.2 0.8 copy-done.1
  3.1 0.0 copy-start.2
  3.1 0.8 copy-done.2
  3.9 0.0 copy-start.3
  3.9 0.8 copy-done.3
  4.7 227.8 %shard_map.75 = (f32[8,16,64]{2,1,0:T(8,128)S(1)}, f32[64,256]{1,0:T(8,128)S(1)}, f32[64,256]{1,0:T(8,128)S(1)}, f32[64,256]{1,0:T(8,128)S(1)}) custom-call(f32[128,16,256]{2,1,0:T(8,128)S(1)} %bitcast.9, f32[64,256]{1,0:T(8,128)S(1)} %bitcast.10, f32[64,256]{1,0:T(8,128)S(1)} %bitcast.11, f32[64,256]{1,0:T(8,128)S(1)} %bitcast.12), custom_call_target="tpu_custom_call" | custom-call | tf_op jit(solution)/shard_map/pallas_call | solution.py:343
  232.5 0.6 copy.12
  233.2 0.6 copy.13
  233.8 0.6 copy.14
  234.4 0.6 copy.15
Async XLA Ops:
  0.6 1.6 copy-start
  2.2 0.8 copy-start.1
  3.1 0.8 copy-start.2
  3.9 0.8 copy-start.3

commit v2 on v1

v2 whole, which is shorter than its diff:
```python
import functools

import jax
import jax.numpy as jnp
from jax import lax
from jax.experimental import pallas as pl
from jax.experimental.pallas import tpu as pltpu
from jax.sharding import PartitionSpec as P

ITERS = 4
MESH = pl.DeviceIdType.MESH
HIGHEST = lax.Precision.HIGHEST
ROUNDS = 11
NEAR = (2, -2, 1, -1)
NEAR_AFTER = 4
Z_STEPS = [8] + [sign * d for d in range(7, 0, -1) for sign in (1, -1)]


def plane_distance(i):
    dx, dy, dc = i % 4, i // 8, (i // 4) % 2
    return min(dx, 4 - dx) + min(dy, 4 - dy) + dc


PLANE_STEPS = sorted(range(1, 32), key=lambda i: -plane_distance(i))


def dot(a, b, ca, cb):
    return lax.dot_general(
        a, b, (((ca,), (cb,)), ((), ())), precision=HIGHEST, preferred_element_type=jnp.float32
    )


def position():
    g = lax.axis_index("gx")
    return lax.axis_index("gy"), (g // 2) % 4, g // 8, g % 2


def device(x, y, z, c):
    return ((z * 4 + y) * 2 + c, x)


def plane_index(x, y, c):
    return (y * 2 + c) * 4 + x


def plane_peer(i, x, y, c):
    return (x + i % 4) % 4, (y + i // 8) % 4, (c + (i // 4) % 2) % 2


def inverse_cholesky(p):
    n = 64
    row = lax.broadcasted_iota(jnp.int32, (n, n), 0)
    col = lax.broadcasted_iota(jnp.int32, (n, n), 1)
    m = jnp.concatenate([p, (row == col).astype(jnp.float32)], axis=1)
    sub = lax.broadcasted_iota(jnp.int32, (8, 128), 0)
    blocks = [m[8 * i : 8 * i + 8, :] for i in range(8)]
    out = []
    for k in range(8):
        cols = {
            (i, j): jnp.broadcast_to(blocks[i][:, 8 * k + j : 8 * k + j + 1], (8, 128))
            for j in range(8)
            for i in range(k, 8)
        }
        rows = [jnp.broadcast_to(blocks[k][j : j + 1, :], (8, 128)) for j in range(8)]
        splat = {
            (r, j): jnp.broadcast_to(cols[k, j][r : r + 1, :], (8, 128))
            for j in range(8)
            for r in range(j, 8)
        }
        for j in range(8):
            scale = lax.rsqrt(splat[j, j])
            for r in range(j + 1, 8):
                splat[r, j] = splat[r, j] * scale
            for i in range(k + 1, 8):
                cols[i, j] = cols[i, j] * scale
            rows[j] = rows[j] * scale
            for t in range(j + 1, 8):
                for r in range(t, 8):
                    splat[r, t] = splat[r, t] - splat[r, j] * splat[t, j]
                for i in range(k + 1, 8):
                    cols[i, t] = cols[i, t] - cols[i, j] * splat[t, j]
                rows[t] = rows[t] - rows[j] * splat[t, j]
        for i in range(k + 1, 8):
            for j in range(8):
                blocks[i] = blocks[i] - cols[i, j] * rows[j]
        done = rows[0]
        for j in range(1, 8):
            done = jnp.where(sub == j, rows[j], done)
        out.append(done)
    return jnp.concatenate(out, axis=0)[:, n:]


def factor(gram, start_t):
    def step(_, block):
        image = dot(block, gram[...], 1, 0)
        return dot(inverse_cholesky(dot(image, image, 1, 1)), image, 1, 0)

    return lax.fori_loop(0, ITERS, step, start_t)


def permutation(kind):
    old = lax.broadcasted_iota(jnp.int32, (256, 256), 0)
    new = lax.broadcasted_iota(jnp.int32, (256, 256), 1)
    if kind == "x":
        source = (new % 128) * 2 + new // 128
    else:
        source = (new % 32) * 8 + new // 32
    return (old == source).astype(jnp.float32)


def swap_blocks(parts):
    lane = lax.broadcasted_iota(jnp.int32, (32, 128), 1) // 16
    parts = list(parts)
    for bit in (1, 2, 4):
        high = (lane & bit) != 0
        new = list(parts)
        for a in range(8):
            if a & bit == 0:
                lo, hi = parts[a], parts[a + bit]
                new[a] = jnp.where(high, pltpu.roll(hi, 16 * bit, 1), lo)
                new[a + bit] = jnp.where(high, hi, pltpu.roll(lo, 128 - 16 * bit, 1))
        parts = new
    return parts


def nothing():
    pass


def all_reduce(g, gram, pieces, r1, r2, part, full, sems, first=nothing, last=nothing):
    x, y, z, c = position()
    own = plane_index(x, y, c)
    row = lax.broadcasted_iota(jnp.int32, (128, 128), 0)
    col = lax.broadcasted_iota(jnp.int32, (128, 128), 1)
    low_right = g[128:, 128:]
    diagonal = jnp.sum(jnp.where(row == col, low_right, 0.0), axis=0, keepdims=True)
    t = jnp.where(row >= col, g[:128, :128], low_right)
    b = g[:128, 128:]
    beside = jnp.broadcast_to(diagonal, (8, 128))
    for q in range(16):
        pieces[q, 0:8] = b[8 * q : 8 * q + 8, :]
        pieces[16 + q, 0:8] = t[8 * q : 8 * q + 8, :]
        pieces[q, 8:16] = beside
        pieces[16 + q, 8:16] = beside
    nine = pl.ds(0, 9)
    for i in PLANE_STEPS:
        tx, ty, tc = plane_peer(i, x, y, c)
        pltpu.make_async_remote_copy(
            pieces.at[plane_index(tx, ty, tc), nine], r1.at[own, nine], sems.at[0], sems.at[1],
            device_id=device(tx, ty, z, tc), device_id_type=MESH,
        ).start()
    r1[own] = pieces[own]
    first()
    plane = r1.at[pl.ds(0, 31), nine]
    pltpu.make_async_copy(plane, plane, sems.at[1]).wait()
    tile, extra = r1[0, 0:8], r1[0, 8:9]
    for i in range(1, 32):
        tile = tile + r1[i, 0:8]
        extra = extra + r1[i, 8:9]
    part[0, 0:8] = tile
    part[0, 8:9] = extra
    for dz in Z_STEPS:
        pltpu.make_async_remote_copy(
            part.at[0, nine], r2.at[z, nine], sems.at[2], sems.at[3],
            device_id=device(x, y, (z + dz + 16) % 16, c), device_id_type=MESH,
        ).start()
    r2[z, 0:8] = tile
    r2[z, 8:9] = extra
    ring = r2.at[pl.ds(0, 15), nine]
    pltpu.make_async_copy(ring, ring, sems.at[3]).wait()
    tile, extra = r2[0, 0:8], r2[0, 8:9]
    for i in range(1, 16):
        tile = tile + r2[i, 0:8]
        extra = extra + r2[i, 8:9]
    part[1, 0:8] = tile
    for i in PLANE_STEPS:
        tx, ty, tc = plane_peer(i, x, y, c)
        pltpu.make_async_remote_copy(
            part.at[1, pl.ds(0, 8)], full.at[own], sems.at[4], sems.at[5],
            device_id=device(tx, ty, z, tc), device_id_type=MESH,
        ).start()
    full[own] = tile
    last()
    pltpu.make_async_copy(plane, plane, sems.at[0]).wait()
    pltpu.make_async_copy(ring, ring, sems.at[2]).wait()
    tiles = full.at[pl.ds(0, 31)]
    pltpu.make_async_copy(tiles, tiles, sems.at[5]).wait()
    b = full[0:16].reshape(128, 128)
    t = full[16:32].reshape(128, 128)
    turned = t.T
    gram[:128, :128] = jnp.where(row >= col, t, turned)
    gram[:128, 128:] = b
    gram[128:, :128] = b.T
    gram[128:, 128:] = jnp.where(row < col, t, jnp.where(row > col, turned, extra))
    pltpu.make_async_copy(tiles, tiles, sems.at[4]).wait()


def kernel(
    x_hbm, sx_hbm, sy_hbm, sz_hbm, core, fx, fy, fz,
    xt, starts, outgoing, by_z, staged, lines, matrix, fc, sc, q, d, at, turned, perm_x, perm_z, vt, halves, gram,
    pieces, r1, r2, part, full, ar_sems, z_recv, near_recv, staged_recv, in_sems, sems,
):
    x, y, z, c = position()
    own = plane_index(x, y, c)
    loads = []
    for half in range(2):
        for rows in range(2):
            block = (pl.ds(64 * rows, 64), slice(None), pl.ds(128 * half, 128))
            loads.append(
                pltpu.make_async_copy(x_hbm.at[block], xt.at[block], in_sems.at[half * 2 + rows])
            )
    for i, start in enumerate((sx_hbm, sy_hbm, sz_hbm)):
        loads.append(pltpu.make_async_copy(start, starts.at[i], in_sems.at[4 + i]))
    for load in loads:
        load.start()
    barrier = pltpu.get_barrier_semaphore()
    for i in PLANE_STEPS:
        tx, ty, tc = plane_peer(i, x, y, c)
        pl.semaphore_signal(barrier, 1, device_id=device(tx, ty, z, tc), device_id_type=MESH)
    for dz in Z_STEPS:
        for dc in range(2):
            pl.semaphore_signal(
                barrier, 1, device_id=device(x, y, (z + dz + 16) % 16, (c + dc) % 2), device_id_type=MESH
            )

    sub = lax.broadcasted_iota(jnp.int32, (8, 128), 0)
    lane = lax.broadcasted_iota(jnp.int32, (8, 128), 1)
    keep = (sub < 4) == (lane < 64)
    for half in range(2):
        loads[2 * half].wait()
        loads[2 * half + 1].wait()
        for s in range(16):
            t = xt[:, s, half * 128 : half * 128 + 128].T
            for zb in range(16):
                tile = t[zb * 8 : zb * 8 + 8, :]
                moved = pltpu.roll(pltpu.roll(tile, 4, 0), 64, 1)
                outgoing[s, half * 16 + zb] = jnp.where(keep, tile, moved)
    pl.semaphore_wait(barrier, 61)

    def distance(k):
        d = 8 - (k + 1) // 2
        return d if k % 2 else -d

    def send_far(k):
        tz = (z + distance(k) + 16) % 16
        pltpu.make_async_remote_copy(
            outgoing.at[tz], by_z.at[z], sems.at[0], z_recv.at[k],
            device_id=device(x, y, tz, c), device_id_type=MESH,
        ).start()

    yc = y * 2 + c
    for k in range(3):
        send_far(k)
    for j, dz in enumerate(NEAR):
        tz = (z + dz + 16) % 16
        for i in PLANE_STEPS:
            tx, ty, tc = plane_peer(i, x, y, c)
            pltpu.make_async_remote_copy(
                outgoing.at[tz, plane_index(tx, ty, tc)], staged.at[j, x, yc],
                sems.at[1], staged_recv.at[j],
                device_id=device(tx, ty, z, tc), device_id_type=MESH,
            ).start()
        staged[j, x, yc] = outgoing[tz, own]
    for k in range(3, ROUNDS):
        send_far(k)

    def forward(buffer, slot):
        for i in PLANE_STEPS:
            tx, ty, tc = plane_peer(i, x, y, c)
            pltpu.make_async_remote_copy(
                buffer.at[slot, plane_index(tx, ty, tc)], lines.at[x, slot * 8 + yc],
                sems.at[1], sems.at[2],
                device_id=device(tx, ty, z, tc), device_id_type=MESH,
            ).start()
        lines[x, slot * 8 + yc] = buffer[slot, own]

    def forward_far(k, carry):
        block = by_z.at[0]
        pltpu.make_async_copy(block, block, z_recv.at[k]).wait()
        d = 8 - (k + 1) // 2
        forward(by_z, (z - d * (2 * (k % 2) - 1) + 16) % 16)
        return carry

    forward(outgoing, z)
    for load in loads[4:]:
        load.wait()
    perm_x[...] = permutation("x")
    perm_z[...] = permutation("z")
    vt[0] = dot(starts[0], perm_x[...], 1, 0)
    vt[1] = dot(starts[2], perm_z[...], 1, 0)

    lax.fori_loop(0, NEAR_AFTER, forward_far, 0)
    for j, dz in enumerate(NEAR):
        tiles = outgoing.at[0, pl.ds(0, 31)]
        pltpu.make_async_copy(tiles, tiles, staged_recv.at[j]).wait()
        tz = (z + dz + 16) % 16
        pltpu.make_async_remote_copy(
            staged.at[j], lines.at[:, pl.ds(z * 8, 8)], sems.at[7], near_recv.at[j],
            device_id=device(x, y, tz, c), device_id_type=MESH,
        ).start()
    lax.fori_loop(NEAR_AFTER, ROUNDS, forward_far, 0)
    tiles = outgoing.at[pl.ds(0, ROUNDS + 1), pl.ds(0, 31)]
    pltpu.make_async_copy(tiles, tiles, sems.at[2]).wait()
    for j in range(len(NEAR)):
        block = staged.at[j]
        pltpu.make_async_copy(block, block, near_recv.at[j]).wait()

    for cx in range(4):
        for zh in range(4):
            for p in range(2):
                matrix[p * 128 : p * 128 + 128, (cx * 4 + zh) * 128 : (cx * 4 + zh + 1) * 128] = (
                    lines[cx, :, p * 4 + zh, :]
                )
    def reduce_gram(k, g, first=nothing, last=nothing):
        all_reduce(
            g, gram, pieces.at[k], r1.at[k], r2.at[k], part.at[k], full.at[k], ar_sems.at[k], first, last
        )

    def sent():
        far = outgoing.at[pl.ds(0, ROUNDS)]
        pltpu.make_async_copy(far, far, sems.at[0]).wait()
        tiles = outgoing.at[:, pl.ds(0, 31)]
        pltpu.make_async_copy(tiles, tiles, sems.at[1]).wait()
        pltpu.make_async_copy(staged, staged, sems.at[7]).wait()

    reduce_gram(0, dot(matrix[...], matrix[...], 1, 1), first=sent)
    vt[2] = factor(gram, vt[0])

    low = lax.broadcasted_iota(jnp.int32, (64, 128), 1) < 64
    for zh in range(4):
        piece = [
            dot(vt[2], matrix[:, (cx * 4 + zh) * 128 : (cx * 4 + zh + 1) * 128], 1, 0)
            for cx in range(4)
        ]
        shifted = [pltpu.roll(v, 64, 1) for v in piece]
        for pair in range(2):
            a, b = 2 * pair, 2 * pair + 1
            for zl, value in (
                (0, jnp.where(low, piece[a], shifted[b])),
                (1, jnp.where(low, shifted[a], piece[b])),
            ):
                zz = zl * 4 + zh
                for kb in range(4):
                    fc[kb * 128 + zz * 16 : kb * 128 + zz * 16 + 16, pair * 128 : pair * 128 + 128] = (
                        value[kb * 16 : kb * 16 + 16, :]
                    )
    def finish_x():
        fx[...] = dot(vt[2], perm_x[...], 1, 1)

    reduce_gram(1, dot(fc[...], fc[...], 0, 0), first=finish_x)
    fy[...] = factor(gram, starts[1])

    for lanes in range(2):
        halves[lanes] = fy[:, lanes * 128 : lanes * 128 + 128]
        for cy in range(4):
            for half in range(2):
                first = (cy * 2 + half) * 8
                vt[2, first : first + 8, lanes * 128 : lanes * 128 + 128] = halves[
                    lanes, pl.ds(32 * half + cy, 8, stride=4), :
                ]
    product = dot(vt[2], fc[...], 1, 1)
    for t in range(8):
        for cx in range(4):
            sc[t * 4 + cx] = product[t * 8 : t * 8 + 8, cx * 128 : cx * 128 + 128]

    for i in range(1, 32):
        tx, ty, tc = plane_peer(i, x, y, c)
        pltpu.make_async_remote_copy(
            sc.at[plane_index(tx, ty, tc)], q.at[own], sems.at[3], sems.at[4],
            device_id=device(tx, ty, z, tc), device_id_type=MESH,
        ).start()
    q[own] = sc[own]
    tiles = sc.at[pl.ds(0, 31)]
    pltpu.make_async_copy(tiles, tiles, sems.at[4]).wait()
    pltpu.make_async_copy(tiles, tiles, sems.at[3]).wait()

    for m in range(8):
        at[1, m * 32 : m * 32 + 32, :] = q[:, m, :]
    lines_z = swap_blocks([at[1, m * 32 : m * 32 + 32, :] for m in range(8)])
    for zz in range(8):
        at[0, zz * 32 : zz * 32 + 32, :] = lines_z[zz]
    tc = z // 8

    def send_lines():
        for m in range(8):
            tz = c * 8 + m

            @pl.when(jnp.logical_or(tz != z, tc != c))
            def _():
                pltpu.make_async_remote_copy(
                    at.at[1, pl.ds(m * 32, 32), :], d.at[z % 8], sems.at[5], sems.at[6],
                    device_id=device(x, y, tz, tc), device_id_type=MESH,
                ).start()

            @pl.when(jnp.logical_and(tz == z, tc == c))
            def _():
                d[z % 8] = at[1, m * 32 : m * 32 + 32, :]

    def take_lines():
        @pl.when(tc == c)
        def _():
            seven = d.at[pl.ds(0, 7)]
            pltpu.make_async_copy(seven, seven, sems.at[6]).wait()
            pltpu.make_async_copy(seven, seven, sems.at[5]).wait()

        @pl.when(tc != c)
        def _():
            pltpu.make_async_copy(d, d, sems.at[6]).wait()
            pltpu.make_async_copy(d, d, sems.at[5]).wait()

        by_zz = swap_blocks([d[s] for s in range(8)])
        for zz in range(8):
            at[0, zz * 32 : zz * 32 + 32, :] = by_zz[zz]
        for half in range(2):
            turned[:, half * 128 : half * 128 + 128] = at[0, half * 128 : half * 128 + 128, :].T

    reduce_gram(2, dot(at[0], at[0], 1, 1), first=send_lines, last=take_lines)
    vt[2] = factor(gram, vt[1])
    result = dot(turned[...], vt[2], 1, 1)
    for s in range(8):
        core[s] = result[s * 16 : s * 16 + 16, :]
    fz[...] = dot(vt[2], perm_z[...], 1, 1)


def write_out(*refs):
    sources, targets, sems = refs[:4], refs[4:8], refs[8]
    copies = [pltpu.make_async_copy(a, b, sems.at[i]) for i, (a, b) in enumerate(zip(sources, targets))]
    for copy in copies:
        copy.start()
    for copy in copies:
        copy.wait()


def local(x_data, start_x, start_y, start_z):
    f32 = jnp.float32
    vmem = pl.BlockSpec(memory_space=pltpu.VMEM)
    hbm = pl.BlockSpec(memory_space=pltpu.HBM)
    xt = jnp.transpose(x_data, (0, 2, 3, 1)).reshape(128, 16, 256)
    shapes = [
        jax.ShapeDtypeStruct((8, 16, 64), f32),
        jax.ShapeDtypeStruct((64, 256), f32),
        jax.ShapeDtypeStruct((64, 256), f32),
        jax.ShapeDtypeStruct((64, 256), f32),
    ]
    results = pl.pallas_call(
        kernel,
        out_shape=shapes,
        in_specs=[hbm] * 4,
        out_specs=[vmem] * 4,
        scratch_shapes=[
            pltpu.VMEM((128, 16, 256), f32),
            pltpu.VMEM((3, 64, 256), f32),
            pltpu.VMEM((16, 32, 8, 128), f32),
            pltpu.VMEM((16, 32, 8, 128), f32),
            pltpu.VMEM((4, 4, 8, 8, 128), f32),
            pltpu.VMEM((4, 128, 8, 128), f32),
            pltpu.VMEM((256, 2048), f32),
            pltpu.VMEM((512, 256), f32),
            pltpu.VMEM((32, 8, 128), f32),
            pltpu.VMEM((32, 8, 128), f32),
            pltpu.VMEM((8, 32, 128), f32),
            pltpu.VMEM((2, 256, 128), f32),
            pltpu.VMEM((128, 256), f32),
            pltpu.VMEM((256, 256), f32),
            pltpu.VMEM((256, 256), f32),
            pltpu.VMEM((3, 64, 256), f32),
            pltpu.VMEM((2, 64, 128), f32),
            pltpu.VMEM((256, 256), f32),
            pltpu.VMEM((3, 32, 16, 128), f32),
            pltpu.VMEM((3, 32, 16, 128), f32),
            pltpu.VMEM((3, 16, 16, 128), f32),
            pltpu.VMEM((3, 2, 16, 128), f32),
            pltpu.VMEM((3, 32, 8, 128), f32),
            pltpu.SemaphoreType.DMA((3, 6)),
            pltpu.SemaphoreType.DMA((ROUNDS,)),
            pltpu.SemaphoreType.DMA((len(NEAR),)),
            pltpu.SemaphoreType.DMA((len(NEAR),)),
            pltpu.SemaphoreType.DMA((7,)),
            pltpu.SemaphoreType.DMA((8,)),
        ],
        compiler_params=pltpu.CompilerParams(
            collective_id=0, has_side_effects=True, vmem_limit_bytes=63 << 20
        ),
    )(xt, start_x.T, start_y.T, start_z.T)
    core, fx, fy, fz = pl.pallas_call(
        write_out,
        out_shape=shapes,
        in_specs=[hbm] * 4,
        out_specs=[hbm] * 4,
        scratch_shapes=[pltpu.SemaphoreType.DMA((4,))],
    )(*results)
    return core, fx.T, fy.T, fz.T


def solution(mesh):
    placed = (P("gx", None, "gy", None), P(), P(), P())
    return jax.shard_map(
        local,
        mesh=mesh,
        in_specs=placed,
        out_specs=(P("gx", "gy", None), P(), P(), P()),
        check_vma=False,
    )
```

time: 235 us -> 218 us (0.928)
  Pallas kernels: 228 us -> 217 us
  local copies, waits for them, and re-layouts: 6.62 us -> 0 us
    pallas_call x1 -> x2, Pallas kernels: 228 us -> 217 us  [the longest x1 208 us: local(): pl.pallas_call(kernel, out_shape=shapes, in_specs=[hbm] * 4, out_specs=[v...]
    unnamed x12 -> x0, local copies, waits for them, and re-layouts: 6.62 us -> none
where the time goes in v2:
time: 218 us
  Pallas kernels  217 us (100%)
    pallas_call x1, Pallas kernels, local(): pl.pallas_call(kernel, out_shape=shapes, in_specs=[hbm] * 4, out_specs=[v...  208 us
    pallas_call x1, Pallas kernels, local(): pl.pallas_call(write_out, out_shape=shapes, in_specs=[hbm] * 4, out_specs...  9.08 us

profile of v2, /device:TPU:1, one launch (start us, length us, event | category | flops | bytes accessed | tf_op | source)
XLA Modules:
  0.0 218.0 jit_solution(16021786668009254775)
XLA Ops:
  0.6 208.1 %shard_map.75 = (f32[8,16,64]{2,1,0:T(8,128)}, f32[64,256]{1,0:T(8,128)}, f32[64,256]{1,0:T(8,128)}, f32[64,256]{1,0:T(8,128)}) custom-call(f32[128,16,256]{2,1,0:T(8,128)} %bitcast.9, f32[64,256]{1,0:T(8,128)} %bitcast.10, f32[64,256]{1,0:T(8,128)} %bitcast.11, f32[64,256]{1,0:T(8,128)} %bitcast.12), custom_call_target="tpu_custom_call" | custom-call | tf_op jit(solution)/shard_map/pallas_call | solution.py:445
  208.8 9.1 %shard_map.76 = (f32[8,16,64]{2,1,0:T(8,128)}, f32[64,256]{1,0:T(8,128)}, f32[64,256]{1,0:T(8,128)}, f32[64,256]{1,0:T(8,128)}) custom-call(f32[8,16,64]{2,1,0:T(8,128)} %get-tuple-element.12.refs_0_, f32[64,256]{1,0:T(8,128)} %get-tuple-element.13.refs_1_, f32[64,256]{1,0:T(8,128)} %get-tuple-element.14.refs_2_, f32[64,256]{1,0:T(8,128)} %get-tuple-element.15.refs_3_), custom_call_target="tpu_custom_call" | custom-call | tf_op jit(solution)/shard_map/pallas_call | solution.py:485

commit v3 on v2

--- a/solution.py
+++ b/solution.py
@@ -12,7 +12,7 @@
 HIGHEST = lax.Precision.HIGHEST
 ROUNDS = 11
 NEAR = (2, -2, 1, -1)
-NEAR_AFTER = 4
+NEAR_AFTER = 8
 Z_STEPS = [8] + [sign * d for d in range(7, 0, -1) for sign in (1, -1)]
 
 
@@ -62,24 +62,16 @@
             for i in range(k, 8)
         }
         rows = [jnp.broadcast_to(blocks[k][j : j + 1, :], (8, 128)) for j in range(8)]
-        splat = {
-            (r, j): jnp.broadcast_to(cols[k, j][r : r + 1, :], (8, 128))
-            for j in range(8)
-            for r in range(j, 8)
-        }
         for j in range(8):
-            scale = lax.rsqrt(splat[j, j])
-            for r in range(j + 1, 8):
-                splat[r, j] = splat[r, j] * scale
-            for i in range(k + 1, 8):
+            scale = lax.rsqrt(jnp.broadcast_to(cols[k, j][j : j + 1, :], (8, 128)))
+            for i in range(k, 8):
                 cols[i, j] = cols[i, j] * scale
             rows[j] = rows[j] * scale
             for t in range(j + 1, 8):
-                for r in range(t, 8):
-                    splat[r, t] = splat[r, t] - splat[r, j] * splat[t, j]
-                for i in range(k + 1, 8):
-                    cols[i, t] = cols[i, t] - cols[i, j] * splat[t, j]
-                rows[t] = rows[t] - rows[j] * splat[t, j]
+                factor_t = jnp.broadcast_to(cols[k, j][t : t + 1, :], (8, 128))
+                for i in range(k, 8):
+                    cols[i, t] = cols[i, t] - cols[i, j] * factor_t
+                rows[t] = rows[t] - rows[j] * factor_t
         for i in range(k + 1, 8):
             for j in range(8):
                 blocks[i] = blocks[i] - cols[i, j] * rows[j]
@@ -205,9 +197,11 @@
     loads = []
     for half in range(2):
         for rows in range(2):
-            block = (pl.ds(64 * rows, 64), slice(None), pl.ds(128 * half, 128))
+            some = pl.ds(64 * rows, 64)
             loads.append(
-                pltpu.make_async_copy(x_hbm.at[block], xt.at[block], in_sems.at[half * 2 + rows])
+                pltpu.make_async_copy(
+                    x_hbm.at[some, :, pl.ds(128 * half, 128)], xt.at[half, some], in_sems.at[half * 2 + rows]
+                )
             )
     for i, start in enumerate((sx_hbm, sy_hbm, sz_hbm)):
         loads.append(pltpu.make_async_copy(start, starts.at[i], in_sems.at[4 + i]))
@@ -226,11 +220,12 @@
     sub = lax.broadcasted_iota(jnp.int32, (8, 128), 0)
     lane = lax.broadcasted_iota(jnp.int32, (8, 128), 1)
     keep = (sub < 4) == (lane < 64)
+    by_row = xt.reshape(2, 2048, 128)
     for half in range(2):
         loads[2 * half].wait()
         loads[2 * half + 1].wait()
         for s in range(16):
-            t = xt[:, s, half * 128 : half * 128 + 128].T
+            t = by_row[half, pl.ds(s, 128, stride=16), :].T
             for zb in range(16):
                 tile = t[zb * 8 : zb * 8 + 8, :]
                 moved = pltpu.roll(pltpu.roll(tile, 4, 0), 64, 1)
@@ -305,11 +300,12 @@
         block = staged.at[j]
         pltpu.make_async_copy(block, block, near_recv.at[j]).wait()
 
+    line_rows = lines.reshape(4, 1024, 128)
     for cx in range(4):
         for zh in range(4):
             for p in range(2):
                 matrix[p * 128 : p * 128 + 128, (cx * 4 + zh) * 128 : (cx * 4 + zh + 1) * 128] = (
-                    lines[cx, :, p * 4 + zh, :]
+                    line_rows[cx, pl.ds(p * 4 + zh, 128, stride=8), :]
                 )
     def reduce_gram(k, g, first=nothing, last=nothing):
         all_reduce(
@@ -375,7 +371,7 @@
     pltpu.make_async_copy(tiles, tiles, sems.at[3]).wait()
 
     for m in range(8):
-        at[1, m * 32 : m * 32 + 32, :] = q[:, m, :]
+        at[1, m * 32 : m * 32 + 32, :] = q.reshape(256, 128)[pl.ds(m, 32, stride=8), :]
     lines_z = swap_blocks([at[1, m * 32 : m * 32 + 32, :] for m in range(8)])
     for zz in range(8):
         at[0, zz * 32 : zz * 32 + 32, :] = lines_z[zz]
@@ -423,11 +419,15 @@
 
 
 def write_out(*refs):
-    sources, targets, sems = refs[:4], refs[4:8], refs[8]
-    copies = [pltpu.make_async_copy(a, b, sems.at[i]) for i, (a, b) in enumerate(zip(sources, targets))]
-    for copy in copies:
+    sources, targets, held, sems = refs[:4], refs[4:8], refs[8:12], refs[12]
+    into = [pltpu.make_async_copy(sources[i], held[i], sems.at[i]) for i in range(4)]
+    out = [pltpu.make_async_copy(held[i], targets[i], sems.at[4 + i]) for i in range(4)]
+    for copy in into:
         copy.start()
-    for copy in copies:
+    for i in range(4):
+        into[i].wait()
+        out[i].start()
+    for copy in out:
         copy.wait()
 
 
@@ -448,7 +448,7 @@
         in_specs=[hbm] * 4,
         out_specs=[vmem] * 4,
         scratch_shapes=[
-            pltpu.VMEM((128, 16, 256), f32),
+            pltpu.VMEM((2, 128, 16, 128), f32),
             pltpu.VMEM((3, 64, 256), f32),
             pltpu.VMEM((16, 32, 8, 128), f32),
             pltpu.VMEM((16, 32, 8, 128), f32),
@@ -487,7 +487,8 @@
         out_shape=shapes,
         in_specs=[hbm] * 4,
         out_specs=[hbm] * 4,
-        scratch_shapes=[pltpu.SemaphoreType.DMA((4,))],
+        scratch_shapes=[pltpu.VMEM(shape.shape, f32) for shape in shapes] + [pltpu.SemaphoreType.DMA((8,))],
+        compiler_params=pltpu.CompilerParams(vmem_limit_bytes=63 << 20),
     )(*results)
     return core, fx.T, fy.T, fz.T
 

time: 218 us -> 209 us (0.959)
  Pallas kernels: 217 us -> 208 us
    pallas_call x1, Pallas kernels: 9.08 us -> 1.63 us  [local(): pl.pallas_call(write_out, out_shape=shapes, in_specs=[hbm] * 4, out_specs...]
where the time goes in v3:
time: 209 us
  Pallas kernels  208 us (100%)
    pallas_call x1, Pallas kernels, local(): pl.pallas_call(kernel, out_shape=shapes, in_specs=[hbm] * 4, out_specs=[v...  206 us

profile of v3, /device:TPU:1, one launch (start us, length us, event | category | flops | bytes accessed | tf_op | source)
XLA Modules:
  0.0 208.7 jit_solution(1474409592385363334)
XLA Ops:
  0.6 206.3 %shard_map.75 = (f32[8,16,64]{2,1,0:T(8,128)}, f32[64,256]{1,0:T(8,128)}, f32[64,256]{1,0:T(8,128)}, f32[64,256]{1,0:T(8,128)}) custom-call(f32[128,16,256]{2,1,0:T(8,128)} %bitcast.9, f32[64,256]{1,0:T(8,128)} %bitcast.10, f32[64,256]{1,0:T(8,128)} %bitcast.11, f32[64,256]{1,0:T(8,128)} %bitcast.12), custom_call_target="tpu_custom_call" | custom-call | tf_op jit(solution)/shard_map/pallas_call | solution.py:445
  206.9 1.6 shard_map.76
